TPU v7x, 32 devices: a whole 2x2x4 slice. The times are simulated.
32 devices in a mesh: space: 4 (over z), work: 8 (over y, x, core).
Axes of the slice: x: 2, y: 2, z: 4, core: 2. Of those that a mesh axis runs over, the one named last changes fastest.
Arguments:
- positions: float32 [3, 32768], P(None, ('space', 'work')), may hold values from -3 to 3
- velocities: float32 [3, 32768], P(None, ('space', 'work')), may hold values from -2 to 2
- masses: float32 [32768], P(('space', 'work')), may hold values from 0.001 to 0.01
- sound2: float32 [32768], P(('space', 'work')), may hold values from 0.1 to 1
- ghost_list: int32 [128, 2], P(('space', 'work')), may hold values from 0 to 7
- dens_list: int32 [256, 6], P(('space', 'work')), may hold values from 0 to 15
- pair_dest: int32 [512, 1], P(('space', 'work')), may hold values from 0 to 7; in each aligned block of 16 rows (0 to 15, 16 to 31, ...) at most 4 rows name the same one
- pair_tiles: int32 [512, 2], P(('space', 'work')), may hold values from 0 to 7
Outputs:
- new_positions: float32 [3, 32768], P(None, ('space', 'work'))
- new_velocities: float32 [3, 32768], P(None, ('space', 'work'))
- acceleration: float32 [3, 32768], P(None, ('space', 'work'))
- density: float32 [32768], P(('space', 'work'))
Inputs may be any that keep to these rules, and one draw needn't show every extreme that they name: `pair_dest`: at most 4 pairs of one device name the same owner; in every draw some device has exactly 4 pairs for one owner.
All inputs are finite; a program needn't handle non-finite values.
Results may differ from a plain program's by a relative error of at most 0.0001.
Values sent between devices are 32-bit elements; how exact they have to be, the bound alone decides.
A program may use at most 64 MiB of HBM per device.

v0:
```python
import functools
import math

import jax
import jax.numpy as jnp
from jax import lax
from jax.experimental import pallas as pl
from jax.experimental.pallas import tpu as pltpu
from jax.sharding import PartitionSpec as P

STEPS = 2
MESH = pl.DeviceIdType.MESH
NT = (((1,), (1,)), ((), ()))
NN = (((1,), (0,)), ((), ()))
LOG2E = math.log2(math.e)
ROOT_LOG2E = math.sqrt(LOG2E)
HIGHEST = lax.Precision.HIGHEST

star_mass = 0.5
softening = 0.1
time_step = 0.1


def inverse(value):
    guess = pl.reciprocal(value, approx=True)
    return guess * (2.0 - value * guess)


def halves(value):
    high = value.astype(jnp.bfloat16)
    return high, (value - high.astype(jnp.float32)).astype(jnp.bfloat16)


def kernel(
    work, space,
    pos_in, vel_in, mass_in, snd_in, ghost_in, dens_in, dest_in, tiles_in,
    result,
    pos, vel, mass, snd, ghost, dens, dest_s, tiles_s, dest_v, tiles_v, load_sem,
    spread, spread_rho, cand, factors, cand_scaled, totals, weights, gathered, moments, sums,
    sector0, sector1, rho0, rho1, ghosts_out0, ghosts_out1, ghosts_in0, ghosts_in1,
    react_out0, react_out1, react_in0, react_in1,
    send_sem, recv_sem, ghost_send, ghost_recv,
):
    tiles = mass.shape[0]
    pairs = dest_v.shape[1]
    ghost_count = ghost.shape[1]
    listed = dens.shape[1]
    unroll = math.gcd(pairs, 4)
    loads = []
    for n, (source, target) in enumerate((
        (pos_in, pos), (vel_in, vel), (mass_in, mass), (snd_in, snd), (ghost_in, ghost),
        (dens_in, dens), (dest_in, dest_s), (tiles_in, tiles_s), (dest_in, dest_v),
        (tiles_in, tiles_v),
    )):
        copy = pltpu.make_async_copy(source, target, load_sem.at[n])
        copy.start()
        loads.append(copy)
    me = lax.axis_index("work")
    here = lax.axis_index("space")
    above, below = lax.rem(here + 1, space), lax.rem(here + space - 1, space)

    barrier = pltpu.get_barrier_semaphore()
    for s in range(1, work):
        pl.semaphore_signal(
            barrier, inc=1, device_id={"work": lax.rem(me + s, work)}, device_id_type=MESH
        )
    for z in (above, below):
        pl.semaphore_signal(barrier, inc=1, device_id={"space": z}, device_id_type=MESH)

    def everyone(step, kind, source, target, own_slot):
        copies = []
        for s in range(1, work):
            to, origin = lax.rem(me + s, work), lax.rem(me + work - s, work)
            if own_slot:
                out, into, arriving = source.at[me], target.at[me], target.at[origin]
            else:
                out, into, arriving = source.at[to], target.at[me], target.at[origin]
            sems = (send_sem.at[step, kind, s - 1], recv_sem.at[step, kind, s - 1])
            copy = pltpu.make_async_remote_copy(
                src_ref=out, dst_ref=into, send_sem=sems[0], recv_sem=sems[1],
                device_id={"work": to}, device_id_type=MESH,
            )
            arrival = pltpu.make_async_remote_copy(
                src_ref=arriving, dst_ref=arriving, send_sem=sems[0], recv_sem=sems[1],
                device_id={"work": to}, device_id_type=MESH,
            )
            copies.append((copy, arrival))
        return copies

    for copy in loads:
        copy.wait()
    masses = mass[...]
    sound2 = snd[...]
    sound = jnp.sqrt(sound2)
    positions, velocities = [], []
    for k in range(3):
        positions.append(
            jnp.concatenate([pos[k : k + 1, 128 * t : 128 * t + 128] for t in range(tiles)], axis=0)
        )
        velocities.append(
            jnp.concatenate([vel[k : k + 1, 128 * t : 128 * t + 128] for t in range(tiles)], axis=0)
        )
    owner_hits = (
        lax.broadcasted_iota(jnp.int32, (work * tiles, pairs), 0)
        == dest_v[...] * tiles + tiles_v[1:2, :]
    ).astype(jnp.float32)
    first_hits = (
        lax.broadcasted_iota(jnp.int32, (tiles, pairs), 0) == tiles_v[0:1, :]
    ).astype(jnp.float32)

    sectors, rhos = (sector0, sector1), (rho0, rho1)
    ghosts_outs, ghosts_ins = (ghosts_out0, ghosts_out1), (ghosts_in0, ghosts_in1)
    react_outs, react_ins = (react_out0, react_out1), (react_in0, react_in1)
    pending = []
    acceleration, density = None, None
    for step in range(STEPS):
        sector, rho, react_out, react_in = sectors[step], rhos[step], react_outs[step], react_ins[step]
        ghosts_out, ghosts_in = ghosts_outs[step], ghosts_ins[step]

        for k in range(3):
            cand[k, 0:tiles, :] = positions[k]
            sector[me, k] = positions[k]
            sector[me, 3 + k] = velocities[k]
        if step == 0:
            cand[3, 0:tiles, :] = masses
            sector[me, 6] = masses
            sector[me, 7] = sound
        for way in range(2):
            for j in range(ghost_count):
                number = ghost[way, j]
                for k in range(4):
                    ghosts_out[way, k * ghost_count + j : k * ghost_count + j + 1, :] = cand[
                        k, pl.ds(number, 1), :
                    ]
        if step == 0:
            pl.semaphore_wait(barrier, work + 1)
        ghost_copies = []
        for way, z in enumerate((above, below)):
            copy = pltpu.make_async_remote_copy(
                src_ref=ghosts_out.at[way], dst_ref=ghosts_in.at[way],
                send_sem=ghost_send.at[step, way], recv_sem=ghost_recv.at[step, way],
                device_id={"space": z}, device_id_type=MESH,
            )
            copy.start()
            ghost_copies.append(copy)
        sector_copies = everyone(step, 0, sector, sector, True)
        for copy, _ in sector_copies:
            copy.start()

        planes = positions + velocities + ([sound] if step == 0 else [])
        blank = jnp.zeros((128 - tiles * len(planes), 128), jnp.float32)
        columns = jnp.concatenate(planes + [blank], axis=0).T
        for q in range(len(planes)):
            for t in range(tiles):
                c = q * tiles + t
                spread[t, q] = jnp.broadcast_to(columns[:, c : c + 1], (128, 128))

        for copy in ghost_copies:
            copy.wait_recv()
        for way in range(2):
            first = tiles + way * ghost_count
            for k in range(4):
                cand[k, first : first + ghost_count, :] = ghosts_in[
                    way, k * ghost_count : (k + 1) * ghost_count, :
                ]

        scaled = [cand[k] * ROOT_LOG2E for k in range(3)]
        mass_log2 = jnp.log2(cand[3])
        for k in range(3):
            cand_scaled[k] = scaled[k]
        cand_scaled[3] = mass_log2

        def density_of(first, carry):
            for t in [first * 2, first * 2 + 1]:
                rows = []
                for c in range(listed + 1):
                    number = t if c == 0 else dens[t, c - 1]
                    rows.append([
                        jnp.broadcast_to(cand_scaled[k, pl.ds(number, 1), :], (32, 128))
                        for k in range(4)
                    ])
                for i in range(0, 128, 32):
                    home = [spread[t, k, i : i + 32, :] * ROOT_LOG2E for k in range(3)]
                    part = None
                    for row in rows:
                        gaps = [home[k] - row[k] for k in range(3)]
                        distance2 = gaps[0] * gaps[0] + gaps[1] * gaps[1] + gaps[2] * gaps[2]
                        term = jnp.exp2(row[3] - distance2)
                        part = term if part is None else part + term
                    totals[t, i : i + 32, :] = part
            return carry

        lax.fori_loop(0, tiles // 2, density_of, 0)
        high, low = halves(totals[...].reshape(tiles * 128, 128))
        ones = jnp.ones((8, 256), jnp.bfloat16)
        row_sums = lax.dot_general(
            ones, jnp.concatenate([high, low], axis=1), NT, preferred_element_type=jnp.float32
        )
        density = jnp.concatenate(
            [row_sums[0:1, 128 * t : 128 * t + 128] for t in range(tiles)], axis=0
        )
        rho[me, 0] = density
        pressure = sound2 / density
        rho[me, 1] = pressure
        rho_copies = everyone(step, 1, rho, rho, True)
        for copy, _ in rho_copies:
            copy.start()
        blank = jnp.zeros((128 - 2 * tiles, 128), jnp.float32)
        columns = jnp.concatenate([density, pressure, blank], axis=0).T
        for q in range(2):
            for t in range(tiles):
                c = q * tiles + t
                spread_rho[t, q] = jnp.broadcast_to(columns[:, c : c + 1], (128, 128))

        for _, arrival in sector_copies:
            arrival.wait_recv()

        def pair_factors(turn, carry):
            for u in range(unroll):
                p = turn * unroll + u
                a, owner, b = tiles_s[0, p], dest_s[0, p], tiles_s[1, p]
                row = [sector[owner, k, pl.ds(b, 1), :] for k in range(6)]
                for k in range(3):
                    gathered[k, pl.ds(p, 1), :] = sector[me, k, pl.ds(a, 1), :]
                    gathered[4 + k, pl.ds(p, 1), :] = row[k]
                gathered[3, pl.ds(p, 1), :] = sector0[me, 6, pl.ds(a, 1), :]
                gathered[7, pl.ds(p, 1), :] = sector0[owner, 6, pl.ds(b, 1), :]
                row.append(sector0[owner, 7, pl.ds(b, 1), :])
                row = [jnp.broadcast_to(value, (32, 128)) for value in row]
                for i in range(0, 128, 32):
                    home = [spread[a, k, i : i + 32, :] for k in range(7)]
                    gaps = [home[k] - row[k] for k in range(3)]
                    distance2 = gaps[0] * gaps[0] + gaps[1] * gaps[1] + gaps[2] * gaps[2]
                    approach = (home[3] - row[3]) * gaps[0]
                    approach = approach + (home[4] - row[4]) * gaps[1]
                    approach = approach + (home[5] - row[5]) * gaps[2]
                    closing = jnp.minimum(approach * inverse(distance2 + 0.01), 0.0)
                    twice = jnp.exp2(1.0 - distance2 * LOG2E)
                    factors[p, 0, i : i + 32, :] = twice
                    factors[p, 1, i : i + 32, :] = (
                        twice * closing * (4.0 * closing - (home[6] + row[6]))
                    )
            return carry

        lax.fori_loop(0, pairs // unroll, pair_factors, 0)
        for side in range(2):
            mass_rows = gathered[4 * side + 3]
            for k in range(4):
                value = mass_rows if k == 3 else mass_rows * gathered[4 * side + k]
                for g in range(3):
                    piece = value.astype(jnp.bfloat16).astype(jnp.float32)
                    value = value - piece
                    moments[side, pl.ds((4 * g + k) * pairs, pairs), :] = piece
        for _, arrival in rho_copies:
            arrival.wait_recv()

        def own_moments(side, p):
            rows = moments[side, pl.ds(p, 12, stride=pairs), :].astype(jnp.bfloat16)
            return jnp.concatenate([rows, rows], axis=1)

        def gains(side):
            moved = [
                sums[side, pl.ds(k * pairs, pairs), :]
                + sums[side, pl.ds((4 + k) * pairs, pairs), :]
                + sums[side, pl.ds((8 + k) * pairs, pairs), :]
                for k in range(4)
            ]
            return [gathered[4 * side + k] * moved[3] - moved[k] for k in range(3)]

        def pair_weights(turn, carry):
            for u in range(unroll):
                p = turn * unroll + u
                a, owner, b = tiles_s[0, p], dest_s[0, p], tiles_s[1, p]
                row_rho = jnp.broadcast_to(rho[owner, 0, pl.ds(b, 1), :], (32, 128))
                row_pressure = jnp.broadcast_to(rho[owner, 1, pl.ds(b, 1), :], (32, 128))
                parts = []
                for i in range(0, 128, 32):
                    own = pl.ds(i, 32)
                    weight = factors[p, 0, own, :] * (spread_rho[a, 1, own, :] + row_pressure)
                    weight = weight + factors[p, 1, own, :] * inverse(
                        spread_rho[a, 0, own, :] + row_rho
                    )
                    high, low = halves(weight)
                    weights[p, 0, own, :] = high
                    weights[p, 1, own, :] = low
                    parts.append((high, low))
                stacked = jnp.concatenate([h for h, _ in parts] + [l for _, l in parts], axis=0)
                sums[1, pl.ds(p, 12, stride=pairs), :] = lax.dot_general(
                    own_moments(0, p), stacked, NN, preferred_element_type=jnp.float32
                )
            return carry

        def first_sums(turn, carry):
            for u in range(unroll):
                p = turn * unroll + u
                sums[0, pl.ds(p, 12, stride=pairs), :] = lax.dot_general(
                    own_moments(1, p),
                    jnp.concatenate([weights[p, 0], weights[p, 1]], axis=1),
                    NT, preferred_element_type=jnp.float32,
                )
            return carry

        lax.fori_loop(0, pairs // unroll, pair_weights, 0)
        for k, value in enumerate(gains(1)):
            reaction = lax.dot_general(
                owner_hits, value, NN, precision=HIGHEST, preferred_element_type=jnp.float32
            )
            for w in range(work):
                react_out[w, k] = reaction[w * tiles : (w + 1) * tiles, :]
        react_copies = everyone(step, 2, react_out, react_in, False)
        for copy, _ in react_copies:
            copy.start()
        lax.fori_loop(0, pairs // unroll, first_sums, 0)
        radius2 = positions[0] * positions[0] + positions[1] * positions[1]
        radius2 = radius2 + positions[2] * positions[2] + softening
        pull = -star_mass / (radius2 * jnp.sqrt(radius2))
        acceleration = []
        for k, value in enumerate(gains(0)):
            gain = lax.dot_general(
                first_hits, value, NN, precision=HIGHEST, preferred_element_type=jnp.float32
            )
            acceleration.append(gain + pull * positions[k] + react_out[me, k])
        for s, (_, arrival) in enumerate(react_copies):
            arrival.wait_recv()
            origin = lax.rem(me + work - (s + 1), work)
            for k in range(3):
                acceleration[k] = acceleration[k] + react_in[origin, k]
        velocities = [velocities[k] + time_step * acceleration[k] for k in range(3)]
        positions = [positions[k] + time_step * velocities[k] for k in range(3)]
        pending = pending + ghost_copies + [
            copy for copy, _ in sector_copies + rho_copies + react_copies
        ]

    for k in range(3):
        result[k] = positions[k]
        result[3 + k] = velocities[k]
        result[6 + k] = acceleration[k]
    result[9] = density
    for copy in pending:
        copy.wait_send()


def unpack(result, new_pos, new_vel, acc_out, den_out):
    den_out[...] = result[9]
    for n, out in enumerate((new_pos, new_vel, acc_out)):
        for k in range(3):
            for t in range(den_out.shape[0]):
                out[k : k + 1, 128 * t : 128 * t + 128] = result[3 * n + k, t : t + 1, :]


def local(positions, velocities, masses, sound2, ghost_list, dens_list, pair_dest, pair_tiles):
    work, space = lax.axis_size("work"), lax.axis_size("space")
    particles = positions.shape[1]
    tiles = particles // 128
    pairs = pair_dest.shape[0]
    ghosts = ghost_list.shape[0]
    vmem = pl.BlockSpec(memory_space=pltpu.VMEM)
    f32 = jnp.float32
    per_step = []
    for shape0, shape1 in (
        ((work, 8, tiles, 128), (work, 6, tiles, 128)),
        ((work, 2, tiles, 128), (work, 2, tiles, 128)),
        ((2, 4 * ghosts, 128), (2, 4 * ghosts, 128)),
        ((2, 4 * ghosts, 128), (2, 4 * ghosts, 128)),
        ((work, 3, tiles, 128), (work, 3, tiles, 128)),
        ((work, 3, tiles, 128), (work, 3, tiles, 128)),
    ):
        per_step += [pltpu.VMEM(shape0, f32), pltpu.VMEM(shape1, f32)]
    i32 = jnp.int32
    packed = pl.pallas_call(
        functools.partial(kernel, work, space),
        out_shape=jax.ShapeDtypeStruct((10, tiles, 128), f32),
        in_specs=[pl.BlockSpec(memory_space=pltpu.HBM)] * 8,
        out_specs=vmem,
        scratch_shapes=[
            pltpu.VMEM((3, particles), f32),
            pltpu.VMEM((3, particles), f32),
            pltpu.VMEM((tiles, 128), f32),
            pltpu.VMEM((tiles, 128), f32),
            pltpu.SMEM((2, ghosts), i32),
            pltpu.SMEM(dens_list.shape, i32),
            pltpu.SMEM((1, pairs), i32),
            pltpu.SMEM((2, pairs), i32),
            pltpu.VMEM((1, pairs), i32),
            pltpu.VMEM((2, pairs), i32),
            pltpu.SemaphoreType.DMA((10,)),
            pltpu.VMEM((tiles, 7, 128, 128), f32),
            pltpu.VMEM((tiles, 2, 128, 128), f32),
            pltpu.VMEM((4, tiles + 2 * ghosts, 128), f32),
            pltpu.VMEM((pairs, 2, 128, 128), f32),
            pltpu.VMEM((4, tiles + 2 * ghosts, 128), f32),
            pltpu.VMEM((tiles, 128, 128), f32),
            pltpu.VMEM((pairs, 2, 128, 128), jnp.bfloat16),
            pltpu.VMEM((8, pairs, 128), f32),
            pltpu.VMEM((2, 12 * pairs, 128), f32),
            pltpu.VMEM((2, 12 * pairs, 128), f32),
            *per_step,
            pltpu.SemaphoreType.DMA((STEPS, 3, work - 1)),
            pltpu.SemaphoreType.DMA((STEPS, 3, work - 1)),
            pltpu.SemaphoreType.DMA((STEPS, 2)),
            pltpu.SemaphoreType.DMA((STEPS, 2)),
        ],
        compiler_params=pltpu.CompilerParams(
            collective_id=0, has_side_effects=True, vmem_limit_bytes=63 * 1024 * 1024
        ),
        name="leapfrog",
    )(
        positions, velocities, masses.reshape(tiles, 128), sound2.reshape(tiles, 128),
        ghost_list.T, dens_list, pair_dest.T, pair_tiles.T,
    )
    wide = jax.ShapeDtypeStruct((3, particles), f32)
    outs = pl.pallas_call(
        unpack,
        out_shape=(wide, wide, wide, jax.ShapeDtypeStruct((tiles, 128), f32)),
        in_specs=[vmem],
        out_specs=(vmem,) * 4,
        name="unpack",
    )(packed)
    return outs[0], outs[1], outs[2], outs[3].reshape(particles)


def solution(mesh):
    return jax.shard_map(
        local,
        mesh=mesh,
        in_specs=(
            P(None, ("space", "work")),
            P(None, ("space", "work")),
            P(("space", "work")),
            P(("space", "work")),
            P(("space", "work"), None),
            P(("space", "work"), None),
            P(("space", "work"), None),
            P(("space", "work"), None),
        ),
        out_specs=(
            P(None, ("space", "work")),
            P(None, ("space", "work")),
            P(None, ("space", "work")),
            P(("space", "work")),
        ),
        check_vma=False,
    )
```

profile of v0, /device:TPU:0, one launch (start us, length us, event | category | flops | bytes accessed | tf_op | source)
XLA Modules:
  0.0 34.9 jit_solution(217623110235253469)
XLA Ops:
  0.6 32.8 %leapfrog.1.result = f32[10,8,128]{2,1,0:T(8,128)} custom-call(f32[3,1024]{1,0:T(4,128)} %pos_in.1, f32[3,1024]{1,0:T(4,128)} %vel_in.1, f32[8,128]{1,0:T(8,128)} %bitcast.6, f32[8,128]{1,0:T(8,128)} %bitcast.7, s32[2,4]{1,0:T(2,128)} %bitcast.8, s32[8,6]{1,0:T(8,128)} %dens_in.1, s32[1,16]{1,0:T(1,128)} %bitcast.10, s32[2,16]{1,0:T(2,128)} %bitcast.9), custom_call_target="tpu_custom_call" | custom-call | tf_op jit(solution)/shard_map/leapfrog/pallas_call | solution.py:370
  33.5 1.4 %unpack.1 = (f32[3,1024]{1,0:T(4,128)}, f32[3,1024]{1,0:T(4,128)}, f32[3,1024]{1,0:T(4,128)}, f32[8,128]{1,0:T(8,128)}) custom-call(f32[10,8,128]{2,1,0:T(8,128)} %leapfrog.1.result), custom_call_target="tpu_custom_call" | custom-call | tf_op jit(solution)/shard_map/unpack/pallas_call | solution.py:412
where the time goes:
time: 35.2 us; the launch traced here: 34.9 us
  Pallas kernels  34.3 us (97%)
  between operations  0.64 us (2%)
    pallas_call x1, Pallas kernels, local(): pl.pallas_call(functools.partial(kernel, work, space), out_shape=jax.Shap...  32.8 us
    pallas_call x1, Pallas kernels, local(): pl.pallas_call(unpack, out_shape=(wide, wide, wide, jax.ShapeDtypeStruct(...  1.42 us

commit v1 on v0

--- a/solution.py
+++ b/solution.py
@@ -36,9 +36,8 @@
     pos_in, vel_in, mass_in, snd_in, ghost_in, dens_in, dest_in, tiles_in,
     result,
     pos, vel, mass, snd, ghost, dens, dest_s, tiles_s, dest_v, tiles_v, load_sem,
-    spread, spread_rho, cand, factors, cand_scaled, totals, weights, gathered, moments, sums,
-    sector0, sector1, rho0, rho1, ghosts_out0, ghosts_out1, ghosts_in0, ghosts_in1,
-    react_out0, react_out1, react_in0, react_in1,
+    spread, spread_rho, cand, factors, totals, weights, gathered, moments, sums,
+    sector, fixed, rho, ghosts_out, ghosts_in, react_out, react_in,
     send_sem, recv_sem, ghost_send, ghost_recv,
 ):
     tiles = mass.shape[0]
@@ -67,7 +66,7 @@
     for z in (above, below):
         pl.semaphore_signal(barrier, inc=1, device_id={"space": z}, device_id_type=MESH)
 
-    def everyone(step, kind, source, target, own_slot):
+    def everyone(kind, source, target, own_slot):
         copies = []
         for s in range(1, work):
             to, origin = lax.rem(me + s, work), lax.rem(me + work - s, work)
@@ -75,7 +74,7 @@
                 out, into, arriving = source.at[me], target.at[me], target.at[origin]
             else:
                 out, into, arriving = source.at[to], target.at[me], target.at[origin]
-            sems = (send_sem.at[step, kind, s - 1], recv_sem.at[step, kind, s - 1])
+            sems = (send_sem.at[kind, s - 1], recv_sem.at[kind, s - 1])
             copy = pltpu.make_async_remote_copy(
                 src_ref=out, dst_ref=into, send_sem=sems[0], recv_sem=sems[1],
                 device_id={"work": to}, device_id_type=MESH,
@@ -92,14 +91,14 @@
     masses = mass[...]
     sound2 = snd[...]
     sound = jnp.sqrt(sound2)
-    positions, velocities = [], []
     for k in range(3):
-        positions.append(
-            jnp.concatenate([pos[k : k + 1, 128 * t : 128 * t + 128] for t in range(tiles)], axis=0)
-        )
-        velocities.append(
-            jnp.concatenate([vel[k : k + 1, 128 * t : 128 * t + 128] for t in range(tiles)], axis=0)
-        )
+        for t in range(tiles):
+            result[k, t : t + 1, :] = pos[k : k + 1, 128 * t : 128 * t + 128]
+            result[3 + k, t : t + 1, :] = vel[k : k + 1, 128 * t : 128 * t + 128]
+    fixed[me, 0] = masses
+    fixed[me, 1] = sound
+    cand[3, 0:tiles, :] = jnp.log2(masses)
+    lanes = lax.broadcasted_iota(jnp.int32, (128, 128), 1)
     owner_hits = (
         lax.broadcasted_iota(jnp.int32, (work * tiles, pairs), 0)
         == dest_v[...] * tiles + tiles_v[1:2, :]
@@ -108,112 +107,119 @@
         lax.broadcasted_iota(jnp.int32, (tiles, pairs), 0) == tiles_v[0:1, :]
     ).astype(jnp.float32)
 
-    sectors, rhos = (sector0, sector1), (rho0, rho1)
-    ghosts_outs, ghosts_ins = (ghosts_out0, ghosts_out1), (ghosts_in0, ghosts_in1)
-    react_outs, react_ins = (react_out0, react_out1), (react_in0, react_in1)
-    pending = []
-    acceleration, density = None, None
-    for step in range(STEPS):
-        sector, rho, react_out, react_in = sectors[step], rhos[step], react_outs[step], react_ins[step]
-        ghosts_out, ghosts_in = ghosts_outs[step], ghosts_ins[step]
-
+    fixed_copies = everyone(3, fixed, fixed, True)
+
+    def one_step(step, carry):
+        positions = [result[k] for k in range(3)]
+        velocities = [result[3 + k] for k in range(3)]
         for k in range(3):
-            cand[k, 0:tiles, :] = positions[k]
+            cand[k, 0:tiles, :] = positions[k] * ROOT_LOG2E
             sector[me, k] = positions[k]
             sector[me, 3 + k] = velocities[k]
-        if step == 0:
-            cand[3, 0:tiles, :] = masses
-            sector[me, 6] = masses
-            sector[me, 7] = sound
         for way in range(2):
             for j in range(ghost_count):
                 number = ghost[way, j]
                 for k in range(4):
-                    ghosts_out[way, k * ghost_count + j : k * ghost_count + j + 1, :] = cand[
+                    ghosts_out[step, way, k * ghost_count + j : k * ghost_count + j + 1, :] = cand[
                         k, pl.ds(number, 1), :
                     ]
-        if step == 0:
+
+        @pl.when(step == 0)
+        def _():
             pl.semaphore_wait(barrier, work + 1)
+
         ghost_copies = []
         for way, z in enumerate((above, below)):
             copy = pltpu.make_async_remote_copy(
-                src_ref=ghosts_out.at[way], dst_ref=ghosts_in.at[way],
+                src_ref=ghosts_out.at[step, way], dst_ref=ghosts_in.at[step, way],
                 send_sem=ghost_send.at[step, way], recv_sem=ghost_recv.at[step, way],
                 device_id={"space": z}, device_id_type=MESH,
             )
             copy.start()
             ghost_copies.append(copy)
-        sector_copies = everyone(step, 0, sector, sector, True)
+        sector_copies = everyone(0, sector, sector, True)
         for copy, _ in sector_copies:
             copy.start()
 
-        planes = positions + velocities + ([sound] if step == 0 else [])
+        @pl.when(step == 0)
+        def _():
+            for copy, _ in fixed_copies:
+                copy.start()
+
+        def gap2(home, row):
+            gaps = [home[k] - row[k] for k in range(3)]
+            return gaps[0] * gaps[0] + gaps[1] * gaps[1] + gaps[2] * gaps[2]
+
+        def wide_row(number):
+            return [
+                jnp.broadcast_to(cand[k, pl.ds(number, 1), :], (32, 128)) for k in range(4)
+            ]
+
+        planes = positions + velocities + [sound]
         blank = jnp.zeros((128 - tiles * len(planes), 128), jnp.float32)
         columns = jnp.concatenate(planes + [blank], axis=0).T
-        for q in range(len(planes)):
-            for t in range(tiles):
-                c = q * tiles + t
-                spread[t, q] = jnp.broadcast_to(columns[:, c : c + 1], (128, 128))
-
+
+        def spread_tile(t, carry):
+            turned = pltpu.roll(columns, lax.rem(128 - t, 128), 1)
+            for q in range(len(planes)):
+                spread[t, q] = jnp.broadcast_to(
+                    turned[:, q * tiles : q * tiles + 1], (128, 128)
+                )
+            row = wide_row(t)
+            for i in range(0, 128, 32):
+                home = [spread[t, k, i : i + 32, :] * ROOT_LOG2E for k in range(3)]
+                totals[t, i : i + 32, :] = jnp.exp2(row[3] - gap2(home, row))
+            return carry
+
+        lax.fori_loop(0, tiles, spread_tile, 0)
         for copy in ghost_copies:
             copy.wait_recv()
         for way in range(2):
             first = tiles + way * ghost_count
             for k in range(4):
                 cand[k, first : first + ghost_count, :] = ghosts_in[
-                    way, k * ghost_count : (k + 1) * ghost_count, :
+                    step, way, k * ghost_count : (k + 1) * ghost_count, :
                 ]
-
-        scaled = [cand[k] * ROOT_LOG2E for k in range(3)]
-        mass_log2 = jnp.log2(cand[3])
-        for k in range(3):
-            cand_scaled[k] = scaled[k]
-        cand_scaled[3] = mass_log2
 
         def density_of(first, carry):
             for t in [first * 2, first * 2 + 1]:
-                rows = []
-                for c in range(listed + 1):
-                    number = t if c == 0 else dens[t, c - 1]
-                    rows.append([
-                        jnp.broadcast_to(cand_scaled[k, pl.ds(number, 1), :], (32, 128))
-                        for k in range(4)
-                    ])
+                rows = [wide_row(dens[t, c]) for c in range(listed)]
                 for i in range(0, 128, 32):
                     home = [spread[t, k, i : i + 32, :] * ROOT_LOG2E for k in range(3)]
-                    part = None
+                    part = totals[t, i : i + 32, :]
                     for row in rows:
-                        gaps = [home[k] - row[k] for k in range(3)]
-                        distance2 = gaps[0] * gaps[0] + gaps[1] * gaps[1] + gaps[2] * gaps[2]
-                        term = jnp.exp2(row[3] - distance2)
-                        part = term if part is None else part + term
-                    totals[t, i : i + 32, :] = part
+                        part = part + jnp.exp2(row[3] - gap2(home, row))
+                    spread_rho[t, 0, i : i + 32, :] = jnp.broadcast_to(
+                        jnp.sum(part, axis=1, keepdims=True), (32, 128)
+                    )
             return carry
 
         lax.fori_loop(0, tiles // 2, density_of, 0)
-        high, low = halves(totals[...].reshape(tiles * 128, 128))
-        ones = jnp.ones((8, 256), jnp.bfloat16)
-        row_sums = lax.dot_general(
-            ones, jnp.concatenate([high, low], axis=1), NT, preferred_element_type=jnp.float32
-        )
-        density = jnp.concatenate(
-            [row_sums[0:1, 128 * t : 128 * t + 128] for t in range(tiles)], axis=0
-        )
+        columns = jnp.zeros((128, 128), jnp.float32)
+        for t in range(tiles):
+            columns = jnp.where(lanes == t, spread_rho[t, 0], columns)
+        density = columns.T[0:tiles, :]
+        result[9] = density
         rho[me, 0] = density
-        pressure = sound2 / density
-        rho[me, 1] = pressure
-        rho_copies = everyone(step, 1, rho, rho, True)
+        rho[me, 1] = sound2 / density
+        rho_copies = everyone(1, rho, rho, True)
         for copy, _ in rho_copies:
             copy.start()
-        blank = jnp.zeros((128 - 2 * tiles, 128), jnp.float32)
-        columns = jnp.concatenate([density, pressure, blank], axis=0).T
-        for q in range(2):
-            for t in range(tiles):
-                c = q * tiles + t
-                spread_rho[t, q] = jnp.broadcast_to(columns[:, c : c + 1], (128, 128))
+
+        def spread_pressure(t, carry):
+            speed = spread[t, 6]
+            spread_rho[t, 1] = speed * speed * inverse(spread_rho[t, 0])
+            return carry
+
+        lax.fori_loop(0, tiles, spread_pressure, 0)
 
         for _, arrival in sector_copies:
             arrival.wait_recv()
+
+        @pl.when(step == 0)
+        def _():
+            for _, arrival in fixed_copies:
+                arrival.wait_recv()
 
         def pair_factors(turn, carry):
             for u in range(unroll):
@@ -223,9 +229,9 @@
                 for k in range(3):
                     gathered[k, pl.ds(p, 1), :] = sector[me, k, pl.ds(a, 1), :]
                     gathered[4 + k, pl.ds(p, 1), :] = row[k]
-                gathered[3, pl.ds(p, 1), :] = sector0[me, 6, pl.ds(a, 1), :]
-                gathered[7, pl.ds(p, 1), :] = sector0[owner, 6, pl.ds(b, 1), :]
-                row.append(sector0[owner, 7, pl.ds(b, 1), :])
+                gathered[3, pl.ds(p, 1), :] = fixed[me, 0, pl.ds(a, 1), :]
+                gathered[7, pl.ds(p, 1), :] = fixed[owner, 0, pl.ds(b, 1), :]
+                row.append(fixed[owner, 1, pl.ds(b, 1), :])
                 row = [jnp.broadcast_to(value, (32, 128)) for value in row]
                 for i in range(0, 128, 32):
                     home = [spread[a, k, i : i + 32, :] for k in range(7)]
@@ -307,7 +313,7 @@
             )
             for w in range(work):
                 react_out[w, k] = reaction[w * tiles : (w + 1) * tiles, :]
-        react_copies = everyone(step, 2, react_out, react_in, False)
+        react_copies = everyone(2, react_out, react_in, False)
         for copy, _ in react_copies:
             copy.start()
         lax.fori_loop(0, pairs // unroll, first_sums, 0)
@@ -325,18 +331,17 @@
             origin = lax.rem(me + work - (s + 1), work)
             for k in range(3):
                 acceleration[k] = acceleration[k] + react_in[origin, k]
-        velocities = [velocities[k] + time_step * acceleration[k] for k in range(3)]
-        positions = [positions[k] + time_step * velocities[k] for k in range(3)]
-        pending = pending + ghost_copies + [
-            copy for copy, _ in sector_copies + rho_copies + react_copies
-        ]
-
-    for k in range(3):
-        result[k] = positions[k]
-        result[3 + k] = velocities[k]
-        result[6 + k] = acceleration[k]
-    result[9] = density
-    for copy in pending:
+        for k in range(3):
+            velocity = velocities[k] + time_step * acceleration[k]
+            result[k] = positions[k] + time_step * velocity
+            result[3 + k] = velocity
+            result[6 + k] = acceleration[k]
+        for copy in ghost_copies + [c for c, _ in sector_copies + rho_copies + react_copies]:
+            copy.wait_send()
+        return carry
+
+    lax.fori_loop(0, STEPS, one_step, 0)
+    for copy, _ in fixed_copies:
         copy.wait_send()
 
 
@@ -356,16 +361,6 @@
     ghosts = ghost_list.shape[0]
     vmem = pl.BlockSpec(memory_space=pltpu.VMEM)
     f32 = jnp.float32
-    per_step = []
-    for shape0, shape1 in (
-        ((work, 8, tiles, 128), (work, 6, tiles, 128)),
-        ((work, 2, tiles, 128), (work, 2, tiles, 128)),
-        ((2, 4 * ghosts, 128), (2, 4 * ghosts, 128)),
-        ((2, 4 * ghosts, 128), (2, 4 * ghosts, 128)),
-        ((work, 3, tiles, 128), (work, 3, tiles, 128)),
-        ((work, 3, tiles, 128), (work, 3, tiles, 128)),
-    ):
-        per_step += [pltpu.VMEM(shape0, f32), pltpu.VMEM(shape1, f32)]
     i32 = jnp.int32
     packed = pl.pallas_call(
         functools.partial(kernel, work, space),
@@ -388,15 +383,20 @@
             pltpu.VMEM((tiles, 2, 128, 128), f32),
             pltpu.VMEM((4, tiles + 2 * ghosts, 128), f32),
             pltpu.VMEM((pairs, 2, 128, 128), f32),
-            pltpu.VMEM((4, tiles + 2 * ghosts, 128), f32),
             pltpu.VMEM((tiles, 128, 128), f32),
             pltpu.VMEM((pairs, 2, 128, 128), jnp.bfloat16),
             pltpu.VMEM((8, pairs, 128), f32),
             pltpu.VMEM((2, 12 * pairs, 128), f32),
             pltpu.VMEM((2, 12 * pairs, 128), f32),
-            *per_step,
-            pltpu.SemaphoreType.DMA((STEPS, 3, work - 1)),
-            pltpu.SemaphoreType.DMA((STEPS, 3, work - 1)),
+            pltpu.VMEM((work, 6, tiles, 128), f32),
+            pltpu.VMEM((work, 2, tiles, 128), f32),
+            pltpu.VMEM((work, 2, tiles, 128), f32),
+            pltpu.VMEM((STEPS, 2, 4 * ghosts, 128), f32),
+            pltpu.VMEM((STEPS, 2, 4 * ghosts, 128), f32),
+            pltpu.VMEM((work, 3, tiles, 128), f32),
+            pltpu.VMEM((work, 3, tiles, 128), f32),
+            pltpu.SemaphoreType.DMA((4, work - 1)),
+            pltpu.SemaphoreType.DMA((4, work - 1)),
             pltpu.SemaphoreType.DMA((STEPS, 2)),
             pltpu.SemaphoreType.DMA((STEPS, 2)),
         ],

time: 35.2 us -> 34.8 us (0.989)
  Pallas kernels: 34.3 us -> 33.9 us
    pallas_call x1, Pallas kernels: 32.8 us -> 32.5 us  [local(): pl.pallas_call(functools.partial(kernel, work, space), out_shape=jax.Shap...]
where the time goes in v1:
time: 34.8 us; the launch traced here: 34.5 us
  Pallas kernels  33.9 us (97%)
  between operations  0.64 us (2%)
    pallas_call x1, Pallas kernels, local(): pl.pallas_call(functools.partial(kernel, work, space), out_shape=jax.Shap...  32.5 us
    pallas_call x1, Pallas kernels, local(): pl.pallas_call(unpack, out_shape=(wide, wide, wide, jax.ShapeDtypeStruct(...  1.42 us

profile of v1, /device:TPU:0, one launch (start us, length us, event | category | flops | bytes accessed | tf_op | source)
XLA Modules:
  0.0 34.5 jit_solution(10918933803008294526)
XLA Ops:
  0.6 32.5 %leapfrog.1.result = f32[10,8,128]{2,1,0:T(8,128)} custom-call(f32[3,1024]{1,0:T(4,128)} %pos_in.1, f32[3,1024]{1,0:T(4,128)} %vel_in.1, f32[8,128]{1,0:T(8,128)} %bitcast.6, f32[8,128]{1,0:T(8,128)} %bitcast.7, s32[2,4]{1,0:T(2,128)} %bitcast.8, s32[8,6]{1,0:T(8,128)} %dens_in.1, s32[1,16]{1,0:T(1,128)} %bitcast.10, s32[2,16]{1,0:T(2,128)} %bitcast.9), custom_call_target="tpu_custom_call" | custom-call | tf_op jit(solution)/shard_map/leapfrog/pallas_call | solution.py:365
  33.1 1.4 %unpack.1 = (f32[3,1024]{1,0:T(4,128)}, f32[3,1024]{1,0:T(4,128)}, f32[3,1024]{1,0:T(4,128)}, f32[8,128]{1,0:T(8,128)}) custom-call(f32[10,8,128]{2,1,0:T(8,128)} %leapfrog.1.result), custom_call_target="tpu_custom_call" | custom-call | tf_op jit(solution)/shard_map/unpack/pallas_call | solution.py:412
